TPU v7x, 256 devices: a whole 4x4x8 slice. The times are simulated.
256 devices in a mesh: row: 32 (over y, x, core), col: 8 (over z).
Axes of the slice: x: 4, y: 4, z: 8, core: 2. Of those that a mesh axis runs over, the one named last changes fastest.
Arguments:
- factor: bfloat16 [256, 32, 128, 128], P('row', 'col'), may hold values from -0.1796875 to 0.1796875
- inverse_pivot: float32 [256, 128], P('row'), may hold values from 0.5 to 2
- lower_rhs: float32 [16, 256, 128], P(None, 'col'), may hold values from -6 to 6
- upper_rhs: float32 [16, 256, 128], P(None, 'col'), may hold values from -6 to 6
- snode_of_block: int32 [256], replicated, may hold values from 0 to 63, as said below
- level_of_snode: int32 [64], replicated, may hold values from 0 to 5, as said below
- slot_columns: int32 [256, 32], P('row', 'col'), may hold values from 0 to 256, as said below
Outputs:
- lower_solution: float32 [16, 256, 128], P(None, 'row')
- upper_solution: float32 [16, 256, 128], P(None, 'row')
Inputs may be any that keep to these rules, and one draw needn't show every extreme that they name: `snode_of_block`: never falling along the blocks, starting at 0 and rising by at most one; every supernode covers an even number of blocks. `level_of_snode`: never falling along the supernodes, starting at 0 and rising by at most one; every level holds one or more supernodes, the top level exactly one, the last. `slot_columns`: the slots of process column c name distinct blocks J with J % 8 == c, or 256; every block row names its own block; a named J lies in the row's supernode or in one that is an ancestor or descendant of it in the elimination tree, in which every supernode below the top level has its parent one level up; some block row fills all 4 slots of some process column.
All inputs are finite; a program needn't handle non-finite values.
Results may differ from a plain program's by a relative error of at most 0.0059.
Values may be sent and summed in bfloat16 or wider, within the bound.
A program may use at most 128 MiB of HBM per device.

v0:
```python
import jax
import jax.numpy as jnp
from jax import lax
from jax.sharding import PartitionSpec as P


def in_one_piece(arrays, axis, dim, along):
    ends, at = ([], 0)
    for a in arrays[:-1]:
        at += a.shape[along]
        ends.append(at)
    both = jnp.concatenate(arrays, axis=along)
    return tuple(jnp.split(lax.all_gather(both, axis, axis=dim, tiled=True), ends, axis=along))


def in_one_piece_2(arrays, axis, split_dim, concat_dim, along):
    ends, at = ([], 0)
    for a in arrays[:-1]:
        at += a.shape[along]
        ends.append(at)
    both = jnp.concatenate(arrays, axis=along)
    return tuple(
        jnp.split(
            lax.all_to_all(both, axis, split_axis=split_dim, concat_axis=concat_dim, tiled=True),
            ends,
            axis=along,
        )
    )


def cut_along(shard, dim, peers):
    before, after = (shard.shape[:dim], shard.shape[dim + 1 :])
    return jnp.moveaxis(shard.reshape(*before, peers, -1, *after), dim, 0)


def sent_and_summed(shard, axis, dim):
    tiles = cut_along(shard, dim, lax.axis_size(axis))
    arrived = lax.all_to_all(tiles, axis, split_axis=0, concat_axis=0, tiled=True)
    return arrived.sum(axis=0)


def in_one_piece_3(arrays, axis, dim, along):
    ends, at = ([], 0)
    for a in arrays[:-1]:
        at += a.shape[along]
        ends.append(at)
    both = jnp.concatenate(arrays, axis=along)
    return tuple(jnp.split(sent_and_summed(both, axis, dim), ends, axis=along))


def rows_first(arrays, axis, dims):
    turned = [jnp.moveaxis(a, dim, 0) for a, dim in zip(arrays, dims)]
    both = jnp.concatenate([t.reshape(len(t), -1) for t in turned], axis=1)
    whole, at, outs = (lax.all_gather(both, axis, axis=0, tiled=True), 0, [])
    for t, dim in zip(turned, dims):
        section = whole[:, at : at + t[0].size].reshape(-1, *t.shape[1:])
        outs.append(jnp.moveaxis(section, 0, dim))
        at += t[0].size
    return tuple(outs)


def owner_slices(lower_piece, upper_piece):
    row_count = lax.axis_size("row")
    col_count = lax.axis_size("col")
    group_count = row_count // col_count
    rhs_count = lower_piece.shape[0]
    rows_here = lower_piece.shape[1]
    share = lower_piece.shape[2]
    gathered = in_one_piece((lower_piece, upper_piece), "row", 1, 0)

    def arrange(values):
        return values.reshape(rhs_count, group_count, col_count, rows_here, share)

    moved = in_one_piece_2((arrange(gathered[0]), arrange(gathered[1])), "col", 2, 4, 0)

    def restore(values):
        whole = values.reshape(rhs_count, group_count, rows_here, share * col_count)
        return jnp.transpose(whole, (0, 2, 1, 3)).reshape(
            rhs_count, rows_here * group_count, share * col_count
        )

    return (restore(moved[0]), restore(moved[1]))


def shards(
    factor, inverse_pivot, lower_rhs, upper_rhs, snode_of_block, level_of_snode, slot_columns
):
    row_count = lax.axis_size("row")
    col_count = lax.axis_size("col")
    row_index = lax.axis_index("row")
    col_index = lax.axis_index("col")
    rows_here = factor.shape[0]
    slots_here = factor.shape[1]
    block_size = factor.shape[2]
    cols_here = lower_rhs.shape[1]
    total_blocks = snode_of_block.shape[0]
    snode_count = level_of_snode.shape[0]
    levels_total = min(6, snode_count // 2)
    group_count = row_count // col_count
    onehot = snode_of_block[:, None] == jnp.arange(snode_count, dtype=jnp.int32)[None, :]
    levels = jnp.sum(jnp.where(onehot, level_of_snode[None, :], 0), axis=1)
    row_ids = jnp.arange(rows_here, dtype=jnp.int32) * row_count + row_index
    col_ids = jnp.arange(cols_here, dtype=jnp.int32) * col_count + col_index
    row_snode = jnp.take(snode_of_block, row_ids)
    row_level = jnp.take(levels, row_ids)
    col_level = jnp.take(levels, col_ids)
    valid = slot_columns < total_blocks
    safe = jnp.minimum(slot_columns, total_blocks - 1)
    slot_snode = jnp.take(snode_of_block, safe)
    slot_level = jnp.take(levels, safe)
    same_snode = row_snode[:, None] == slot_snode
    lower_mask = valid & jnp.where(
        same_snode, safe < row_ids[:, None], row_level[:, None] > slot_level
    )
    upper_mask = valid & jnp.where(
        same_snode, safe > row_ids[:, None], row_level[:, None] < slot_level
    )
    diagonal = valid & (safe == row_ids[:, None])
    local_cols = (safe // col_count).reshape(-1)
    inner_ids = jnp.arange(block_size, dtype=jnp.int32)
    strict_lower = inner_ids[None, :] < inner_ids[:, None]
    strict_upper = inner_ids[None, :] > inner_ids[:, None]
    lower_keep = jnp.where(
        diagonal[:, :, None, None], strict_lower[None, None], lower_mask[:, :, None, None]
    )
    upper_keep = jnp.where(
        diagonal[:, :, None, None], strict_upper[None, None], upper_mask[:, :, None, None]
    )
    zero_value = jnp.zeros((), factor.dtype)
    lower_op = jnp.where(lower_keep, factor, zero_value)
    upper_op = jnp.where(upper_keep, factor, zero_value)
    diag_weight = (row_index % col_count == col_index).astype(jnp.float32)
    diag_slot = row_index // col_count

    def diagonal_part(values):
        reshaped = values.reshape(values.shape[0], rows_here, group_count, block_size)
        return lax.dynamic_index_in_dim(reshaped, diag_slot, 2, keepdims=False).astype(jnp.float32)

    def picked(values):
        taken = jnp.take(values, local_cols, axis=1)
        return taken.reshape(values.shape[0], rows_here, slots_here, block_size)

    def products(lower_in, upper_in):
        lower_part = jnp.einsum(
            "kisb,isab->kia", picked(lower_in), lower_op, preferred_element_type=jnp.float32
        )
        upper_part = jnp.einsum(
            "kisb,isab->kia", picked(upper_in), upper_op, preferred_element_type=jnp.float32
        )
        lower_part = lower_part + diag_weight * diagonal_part(lower_in)
        upper_part = upper_part + diag_weight * inverse_pivot[None, :, :] * diagonal_part(upper_in)
        return in_one_piece_3((lower_part, upper_part), "col", 2, 0)

    def spread(lower_piece, upper_piece):
        return owner_slices(lower_piece, upper_piece)

    share_width = block_size // col_count
    lower_res = lower_rhs
    upper_res = upper_rhs
    lower_sol = jnp.zeros((lower_rhs.shape[0], rows_here, share_width), jnp.float32)
    upper_sol = jnp.zeros((upper_rhs.shape[0], rows_here, share_width), jnp.float32)
    for level_step in range(levels_total):
        upper_level = levels_total - 1 - level_step
        lower_in = jnp.where((col_level == level_step)[None, :, None], lower_res, 0.0).astype(
            jnp.bfloat16
        )
        upper_in = jnp.where((col_level == upper_level)[None, :, None], upper_res, 0.0).astype(
            jnp.bfloat16
        )
        lower_sum, upper_sum = products(lower_in, upper_in)
        lower_new = jnp.where((row_level == level_step)[None, :, None], lower_sum, 0.0)
        upper_new = jnp.where((row_level == upper_level)[None, :, None], upper_sum, 0.0)
        lower_sol = lower_sol + lower_new
        upper_sol = upper_sol + upper_new
        if level_step + 1 < levels_total:
            lower_cols, upper_cols = spread(
                lower_new.astype(jnp.bfloat16), upper_new.astype(jnp.bfloat16)
            )
            lower_upd, upper_upd = products(lower_cols, upper_cols)
            lower_back = jnp.where((row_level > level_step)[None, :, None], lower_upd, 0.0).astype(
                jnp.bfloat16
            )
            upper_back = jnp.where((row_level < upper_level)[None, :, None], upper_upd, 0.0).astype(
                jnp.bfloat16
            )
            lower_moved, upper_moved = spread(lower_back, upper_back)
            lower_res = lower_res - lower_moved.astype(jnp.float32)
            upper_res = upper_res - upper_moved.astype(jnp.float32)
    lower_sol, upper_sol = rows_first((lower_sol, upper_sol), "col", (2, 2))
    return (lower_sol, upper_sol)


def solution(mesh):
    in_specs = (
        P("row", "col", None, None),
        P("row", None),
        P(None, "col", None),
        P(None, "col", None),
        P(),
        P(),
        P("row", "col"),
    )
    out_specs = (P(None, "row", None), P(None, "row", None))
    return jax.shard_map(shards, mesh=mesh, in_specs=in_specs, out_specs=out_specs, check_vma=False)
```

profile of v0, /device:TPU:1, one launch (start us, length us, event | category | flops | bytes accessed | tf_op | source)
XLA Modules:
  0.0 764.2 jit_solution(218094547411540907)
XLA Ops:
  31.4 27.4 %all_gather.33 = bf16[32,256,16]{0,2,1:T(8,128)(2,1)S(1)} all-gather(bf16[32,8,16]{0,2,1:T(8,128)(2,1)S(1)} %pad_maximum_fusion.21), channel_id=1, replica_groups=mesh['row'=32,'col'=8] {'row'}, dimensions={1}, use_global_device_ids=true | all-gather | bytes 270336 | tf_op jit(solution)/shard_map/all_gather | solution.py:13
  68.7 14.9 %all_to_all.205 = bf16[8,2,8192]{2,1,0:T(2,128)(2,1)S(1)} all-to-all(bf16[8,2,8192]{2,1,0:T(2,128)(2,1)S(1)} %reshape.1027), channel_id=1, replica_groups=mesh['row'=32,'col'=8] {'col'}, dimensions={0} | all-to-all | bytes 524288 | tf_op jit(solution)/shard_map/all_to_all | solution.py:24
  90.9 10.6 %all_to_all.206 = f32[8,1,4096]{2,1,0:T(1,128)S(1)} all-to-all(f32[8,1,4096]{2,1,0:T(1,128)S(1)} %reshape.1029), channel_id=1, replica_groups=mesh['row'=32,'col'=8] {'col'}, dimensions={0} | all-to-all | bytes 262144 | tf_op jit(solution)/shard_map/all_to_all | solution.py:38
  102.8 25.9 %all_gather.34 = bf16[32,256,16]{0,2,1:T(8,128)(2,1)S(1)} all-gather(bf16[32,8,16]{0,2,1:T(8,128)(2,1)S(1)} %pad_maximum_fusion.22), channel_id=1, replica_groups=mesh['row'=32,'col'=8] {'row'}, dimensions={1}, use_global_device_ids=true | all-gather | bytes 270336 | tf_op jit(solution)/shard_map/all_gather | solution.py:13
  130.8 15.0 %all_to_all.207 = bf16[8,2,8192]{2,1,0:T(2,128)(2,1)S(1)} all-to-all(bf16[8,2,8192]{2,1,0:T(2,128)(2,1)S(1)} %reshape.1031), channel_id=1, replica_groups=mesh['row'=32,'col'=8] {'col'}, dimensions={0} | all-to-all | bytes 524288 | tf_op jit(solution)/shard_map/all_to_all | solution.py:24
  162.9 10.6 %all_to_all.208 = f32[8,1,4096]{2,1,0:T(1,128)S(1)} all-to-all(f32[8,1,4096]{2,1,0:T(1,128)S(1)} %reshape.1033), channel_id=1, replica_groups=mesh['row'=32,'col'=8] {'col'}, dimensions={0} | all-to-all | bytes 262144 | tf_op jit(solution)/shard_map/all_to_all | solution.py:38
  174.8 24.8 %all_gather.35 = bf16[32,256,16]{0,2,1:T(8,128)(2,1)S(1)} all-gather(bf16[32,8,16]{0,2,1:T(8,128)(2,1)S(1)} %pad_maximum_fusion.23), channel_id=1, replica_groups=mesh['row'=32,'col'=8] {'row'}, dimensions={1}, use_global_device_ids=true | all-gather | bytes 270336 | tf_op jit(solution)/shard_map/all_gather | solution.py:13
  209.5 14.8 %all_to_all.209 = bf16[8,2,8192]{2,1,0:T(2,128)(2,1)S(1)} all-to-all(bf16[8,2,8192]{2,1,0:T(2,128)(2,1)S(1)} %reshape.1035), channel_id=1, replica_groups=mesh['row'=32,'col'=8] {'col'}, dimensions={0} | all-to-all | bytes 524288 | tf_op jit(solution)/shard_map/all_to_all | solution.py:24
  231.5 10.6 %all_to_all.210 = f32[8,1,4096]{2,1,0:T(1,128)S(1)} all-to-all(f32[8,1,4096]{2,1,0:T(1,128)S(1)} %reshape.1037), channel_id=1, replica_groups=mesh['row'=32,'col'=8] {'col'}, dimensions={0} | all-to-all | bytes 262144 | tf_op jit(solution)/shard_map/all_to_all | solution.py:38
  243.5 26.1 %all_gather.36 = bf16[32,256,16]{0,2,1:T(8,128)(2,1)S(1)} all-gather(bf16[32,8,16]{0,2,1:T(8,128)(2,1)S(1)} %pad_maximum_fusion.24), channel_id=1, replica_groups=mesh['row'=32,'col'=8] {'row'}, dimensions={1}, use_global_device_ids=true | all-gather | bytes 270336 | tf_op jit(solution)/shard_map/all_gather | solution.py:13
  271.6 14.8 %all_to_all.211 = bf16[8,2,8192]{2,1,0:T(2,128)(2,1)S(1)} all-to-all(bf16[8,2,8192]{2,1,0:T(2,128)(2,1)S(1)} %reshape.1039), channel_id=1, replica_groups=mesh['row'=32,'col'=8] {'col'}, dimensions={0} | all-to-all | bytes 524288 | tf_op jit(solution)/shard_map/all_to_all | solution.py:24
  315.9 24.6 %all_gather.37 = bf16[32,256,16]{0,2,1:T(8,128)(2,1)S(1)} all-gather(bf16[32,8,16]{0,2,1:T(8,128)(2,1)S(1)} %pad_maximum_fusion.25), channel_id=1, replica_groups=mesh['row'=32,'col'=8] {'row'}, dimensions={1}, use_global_device_ids=true | all-gather | bytes 270336 | tf_op jit(solution)/shard_map/all_gather | solution.py:13
  350.4 14.8 %all_to_all.213 = bf16[8,2,8192]{2,1,0:T(2,128)(2,1)S(1)} all-to-all(bf16[8,2,8192]{2,1,0:T(2,128)(2,1)S(1)} %reshape.1043), channel_id=1, replica_groups=mesh['row'=32,'col'=8] {'col'}, dimensions={0} | all-to-all | bytes 524288 | tf_op jit(solution)/shard_map/all_to_all | solution.py:24
  384.3 26.3 %all_gather.38 = bf16[32,256,16]{0,2,1:T(8,128)(2,1)S(1)} all-gather(bf16[32,8,16]{0,2,1:T(8,128)(2,1)S(1)} %pad_maximum_fusion.26), channel_id=1, replica_groups=mesh['row'=32,'col'=8] {'row'}, dimensions={1}, use_global_device_ids=true | all-gather | bytes 270336 | tf_op jit(solution)/shard_map/all_gather | solution.py:13
  412.7 14.8 %all_to_all.215 = bf16[8,2,8192]{2,1,0:T(2,128)(2,1)S(1)} all-to-all(bf16[8,2,8192]{2,1,0:T(2,128)(2,1)S(1)} %reshape.1047), channel_id=1, replica_groups=mesh['row'=32,'col'=8] {'col'}, dimensions={0} | all-to-all | bytes 524288 | tf_op jit(solution)/shard_map/all_to_all | solution.py:24
  460.2 24.5 %all_gather.39 = bf16[32,256,16]{0,2,1:T(8,128)(2,1)S(1)} all-gather(bf16[32,8,16]{0,2,1:T(8,128)(2,1)S(1)} %pad_maximum_fusion.27), channel_id=1, replica_groups=mesh['row'=32,'col'=8] {'row'}, dimensions={1}, use_global_device_ids=true | all-gather | bytes 270336 | tf_op jit(solution)/shard_map/all_gather | solution.py:13
  494.7 14.8 %all_to_all.217 = bf16[8,2,8192]{2,1,0:T(2,128)(2,1)S(1)} all-to-all(bf16[8,2,8192]{2,1,0:T(2,128)(2,1)S(1)} %reshape.1051), channel_id=1, replica_groups=mesh['row'=32,'col'=8] {'col'}, dimensions={0} | all-to-all | bytes 524288 | tf_op jit(solution)/shard_map/all_to_all | solution.py:24
  529.7 26.1 %all_gather.40 = bf16[32,256,16]{0,2,1:T(8,128)(2,1)S(1)} all-gather(bf16[32,8,16]{0,2,1:T(8,128)(2,1)S(1)} %pad_maximum_fusion.28), channel_id=1, replica_groups=mesh['row'=32,'col'=8] {'row'}, dimensions={1}, use_global_device_ids=true | all-gather | bytes 270336 | tf_op jit(solution)/shard_map/all_gather | solution.py:13
  557.8 14.8 %all_to_all.219 = bf16[8,2,8192]{2,1,0:T(2,128)(2,1)S(1)} all-to-all(bf16[8,2,8192]{2,1,0:T(2,128)(2,1)S(1)} %reshape.1055), channel_id=1, replica_groups=mesh['row'=32,'col'=8] {'col'}, dimensions={0} | all-to-all | bytes 524288 | tf_op jit(solution)/shard_map/all_to_all | solution.py:24
  602.7 24.7 %all_gather.41 = bf16[32,256,16]{0,2,1:T(8,128)(2,1)S(1)} all-gather(bf16[32,8,16]{0,2,1:T(8,128)(2,1)S(1)} %pad_maximum_fusion.29), channel_id=1, replica_groups=mesh['row'=32,'col'=8] {'row'}, dimensions={1}, use_global_device_ids=true | all-gather | bytes 270336 | tf_op jit(solution)/shard_map/all_gather | solution.py:13
  637.4 14.8 %all_to_all.221 = bf16[8,2,8192]{2,1,0:T(2,128)(2,1)S(1)} all-to-all(bf16[8,2,8192]{2,1,0:T(2,128)(2,1)S(1)} %reshape.1059), channel_id=1, replica_groups=mesh['row'=32,'col'=8] {'col'}, dimensions={0} | all-to-all | bytes 524288 | tf_op jit(solution)/shard_map/all_to_all | solution.py:24
  671.3 26.0 %all_gather.42 = bf16[32,256,16]{0,2,1:T(8,128)(2,1)S(1)} all-gather(bf16[32,8,16]{0,2,1:T(8,128)(2,1)S(1)} %pad_maximum_fusion.30), channel_id=1, replica_groups=mesh['row'=32,'col'=8] {'row'}, dimensions={1}, use_global_device_ids=true | all-gather | bytes 270336 | tf_op jit(solution)/shard_map/all_gather | solution.py:13
  699.4 14.8 %all_to_all.223 = bf16[8,2,8192]{2,1,0:T(2,128)(2,1)S(1)} all-to-all(bf16[8,2,8192]{2,1,0:T(2,128)(2,1)S(1)} %reshape.1063), channel_id=1, replica_groups=mesh['row'=32,'col'=8] {'col'}, dimensions={0} | all-to-all | bytes 524288 | tf_op jit(solution)/shard_map/all_to_all | solution.py:24
  744.2 18.3 %all_gather.43 = f32[128,256]{1,0:T(8,128)S(1)} all-gather(f32[16,256]{1,0:T(8,128)S(1)} %pad_maximum_fusion.31), channel_id=1, replica_groups=mesh['row'=32,'col'=8] {'col'}, dimensions={0}, use_global_device_ids=true | all-gather | bytes 147456 | tf_op jit(solution)/shard_map/all_gather | solution.py:54
  (606 shorter events, 305.2 us)
Async XLA Ops:
  12.8 16.8 %all-to-all-start = ((f32[8,1,4096]{2,1,0:T(1,128)}), f32[8,1,4096]{2,1,0:T(1,128)S(1)}, u32[]{:S(2)}, u32[]{:S(2)}) async-start(f32[8,1,4096]{2,1,0:T(1,128)} %reshape.1025), calls=%async_computation | async-start | bytes 262144 | tf_op jit(solution)/shard_map/all_to_all | solution.py:38
  22.4 36.8 %copy-start.54 = (pred[8]{0:T(512)(128)(4,1)}, pred[8]{0:T(512)(128)(4,1)S(1)}, u32[]{:S(2)}) copy-start(pred[8]{0:T(512)(128)(4,1)S(1)} %get-tuple-element.95) | copy-start | bytes 28
  22.4 36.8 %copy-start.56 = (pred[8]{0:T(512)(128)(4,1)}, pred[8]{0:T(512)(128)(4,1)S(1)}, u32[]{:S(2)}) copy-start(pred[8]{0:T(512)(128)(4,1)S(1)} %get-tuple-element.98) | copy-start | bytes 28
  90.3 12.3 %copy-start.86 = (pred[8]{0:T(512)(128)(4,1)S(1)}, pred[8]{0:T(512)(128)(4,1)}, u32[]{:S(2)}) copy-start(pred[8]{0:T(512)(128)(4,1)} %get-tuple-element.94) | copy-start | bytes 28
  90.4 12.3 %copy-start.87 = (pred[8]{0:T(512)(128)(4,1)S(1)}, pred[8]{0:T(512)(128)(4,1)}, u32[]{:S(2)}) copy-start(pred[8]{0:T(512)(128)(4,1)} %get-tuple-element.96) | copy-start | bytes 28
  162.4 12.3 %copy-start.51 = (pred[8]{0:T(512)(128)(4,1)S(1)}, pred[8]{0:T(512)(128)(4,1)}, u32[]{:S(2)}) copy-start(pred[8]{0:T(512)(128)(4,1)} %get-tuple-element.97) | copy-start | bytes 28
  231.0 12.3 %copy-start.84 = (pred[8]{0:T(512)(128)(4,1)S(1)}, pred[8]{0:T(512)(128)(4,1)}, u32[]{:S(2)}) copy-start(pred[8]{0:T(512)(128)(4,1)} %get-tuple-element.90) | copy-start | bytes 28
  231.0 12.3 %copy-start.85 = (pred[8]{0:T(512)(128)(4,1)S(1)}, pred[8]{0:T(512)(128)(4,1)}, u32[]{:S(2)}) copy-start(pred[8]{0:T(512)(128)(4,1)} %get-tuple-element.92) | copy-start | bytes 28
  303.0 12.3 %copy-start.48 = (pred[8]{0:T(512)(128)(4,1)S(1)}, pred[8]{0:T(512)(128)(4,1)}, u32[]{:S(2)}) copy-start(pred[8]{0:T(512)(128)(4,1)} %get-tuple-element.93) | copy-start | bytes 28
  371.9 12.3 %copy-start.82 = (pred[8]{0:T(512)(128)(4,1)S(1)}, pred[8]{0:T(512)(128)(4,1)}, u32[]{:S(2)}) copy-start(pred[8]{0:T(512)(128)(4,1)} %get-tuple-element.87) | copy-start | bytes 28
  371.9 12.3 %copy-start.83 = (pred[8]{0:T(512)(128)(4,1)S(1)}, pred[8]{0:T(512)(128)(4,1)}, u32[]{:S(2)}) copy-start(pred[8]{0:T(512)(128)(4,1)} %get-tuple-element.88) | copy-start | bytes 28
  447.3 12.3 %copy-start.49 = (pred[8]{0:T(512)(128)(4,1)S(1)}, pred[8]{0:T(512)(128)(4,1)}, u32[]{:S(2)}) copy-start(pred[8]{0:T(512)(128)(4,1)} %get-tuple-element.93) | copy-start | bytes 28
  517.2 12.3 %copy-start.80 = (pred[8]{0:T(512)(128)(4,1)S(1)}, pred[8]{0:T(512)(128)(4,1)}, u32[]{:S(2)}) copy-start(pred[8]{0:T(512)(128)(4,1)} %get-tuple-element.85) | copy-start | bytes 28
  517.2 12.3 %copy-start.81 = (pred[8]{0:T(512)(128)(4,1)S(1)}, pred[8]{0:T(512)(128)(4,1)}, u32[]{:S(2)}) copy-start(pred[8]{0:T(512)(128)(4,1)} %get-tuple-element.86) | copy-start | bytes 28
  589.8 12.3 %copy-start.52 = (pred[8]{0:T(512)(128)(4,1)S(1)}, pred[8]{0:T(512)(128)(4,1)}, u32[]{:S(2)}) copy-start(pred[8]{0:T(512)(128)(4,1)} %get-tuple-element.97) | copy-start | bytes 28
  658.8 12.3 %copy-start.79 = (pred[8]{0:T(512)(128)(4,1)S(1)}, pred[8]{0:T(512)(128)(4,1)}, u32[]{:S(2)}) copy-start(pred[8]{0:T(512)(128)(4,1)} %get-tuple-element.84) | copy-start | bytes 28
  658.8 12.3 %copy-start.88 = (pred[8]{0:T(512)(128)(4,1)S(1)}, pred[8]{0:T(512)(128)(4,1)}, u32[]{:S(2)}) copy-start(pred[8]{0:T(512)(128)(4,1)} %get-tuple-element.4) | copy-start | bytes 28
  731.2 12.3 %copy-start.23 = (f32[32,8,16]{0,2,1:T(8,128)S(1)}, f32[32,8,16]{0,2,1:T(8,128)}, u32[]{:S(2)}) copy-start(f32[32,8,16]{0,2,1:T(8,128)} %copy-done.22) | copy-start | bytes 49156
  731.2 12.3 %copy-start.25 = (f32[32,8,16]{0,2,1:T(8,128)S(1)}, f32[32,8,16]{0,2,1:T(8,128)}, u32[]{:S(2)}) copy-start(f32[32,8,16]{0,2,1:T(8,128)} %copy-done.24) | copy-start | bytes 49156
  731.3 12.3 %copy-start.27 = (f32[32,8,16]{0,2,1:T(8,128)S(1)}, f32[32,8,16]{0,2,1:T(8,128)}, u32[]{:S(2)}) copy-start(f32[32,8,16]{0,2,1:T(8,128)} %copy-done.26) | copy-start | bytes 49156
  731.3 12.3 %copy-start.50 = (pred[8]{0:T(512)(128)(4,1)S(1)}, pred[8]{0:T(512)(128)(4,1)}, u32[]{:S(2)}) copy-start(pred[8]{0:T(512)(128)(4,1)} %get-tuple-element.93) | copy-start | bytes 28
  731.3 12.3 %copy-start.53 = (pred[8]{0:T(512)(128)(4,1)S(1)}, pred[8]{0:T(512)(128)(4,1)}, u32[]{:S(2)}) copy-start(pred[8]{0:T(512)(128)(4,1)} %get-tuple-element.97) | copy-start | bytes 28
  731.3 12.3 %copy-start.55 = (pred[8]{0:T(512)(128)(4,1)S(1)}, pred[8]{0:T(512)(128)(4,1)}, u32[]{:S(2)}) copy-start(pred[8]{0:T(512)(128)(4,1)} %copy-done.54) | copy-start | bytes 28
  731.3 12.3 %copy-start.57 = (pred[8]{0:T(512)(128)(4,1)S(1)}, pred[8]{0:T(512)(128)(4,1)}, u32[]{:S(2)}) copy-start(pred[8]{0:T(512)(128)(4,1)} %copy-done.56) | copy-start | bytes 28
  (107 other events, 243.8 us)
where the time goes:
time: 778 us; the launch traced here: 764 us
  blocking collectives  529 us (68%)
  local copies, waits for them, and re-layouts  160 us (21%)
  other arithmetic  42.1 us (5%)
  matrix products  12.2 us (2%)
  starting transfers between devices  9.02 us (1%)
    all_gather x10, blocking collectives, in_one_piece(): lax.all_gather(both, axis, axis=dim, tiled=True)  256 us
    all_to_all x10, blocking collectives, in_one_piece_2(): lax.all_to_all(both, axis, split_axis=split_dim, concat_axis=concat_dim,...  148 us
    all_to_all x10, blocking collectives, sent_and_summed(): lax.all_to_all(tiles, axis, split_axis=0, concat_axis=0, tiled=True)  106 us
    unnamed x315, local copies, waits for them, and re-layouts  47.7 us
    convert_element_type x15, local copies, waits for them, and re-layouts, shards(): lower_res = lower_res - lower_moved.astype(jnp.float32)  30.6 us
    convert_element_type x15, local copies, waits for them, and re-layouts, shards(): upper_res = upper_res - upper_moved.astype(jnp.float32)  25.4 us
    all_gather x1, blocking collectives, rows_first(): whole, at, outs = (lax.all_gather(both, axis, axis=0, tiled=True), 0, [])  18.3 us
  transfers between devices with their start and end apart: 1, of which 1 were waited for; matrix products, arithmetic and copies ran while one was open for 0% of the time, Pallas kernels for 0%

commit v1 on v0

v1 whole, which is shorter than its diff:
```python
import functools

import jax
import jax.numpy as jnp
from jax import lax
from jax.experimental import pallas as pl
from jax.experimental.pallas import tpu as pltpu
from jax.sharding import PartitionSpec as P

MESH = pl.DeviceIdType.MESH
LEVELS = 6
ROUNDS = 2 * LEVELS - 1
NT = (((1,), (1,)), ((), ()))


def kernel(
    dims, tbl, flt, f_ref, v0_ref, own_ref, piv_ref, low_ref, up_ref,
    f2, held, land, psend, precv, xs, xrecv, send1, recv1, send2, recv2, send3, recv3,
):
    rows, cols, nrow, nslot, ncol = dims
    per = rows // cols
    zero = ROUNDS * ncol
    n_tbl = ROUNDS * nrow * nslot
    row, col = lax.axis_index("row"), lax.axis_index("col")
    base, lane = (row // cols) * cols, row % cols
    on_diag = col == lane
    own_pos = row // cols + per * (row % cols)

    def dest(i):
        return (base + i, lane)

    def source(c):
        return (base + col, c)

    barrier = pltpu.get_barrier_semaphore()

    def plane(body):
        def step(k, carry):
            body(lax.rem(row + k, rows))
            return carry

        lax.fori_loop(1, rows, step, 0)

    def across(body):
        def step(k, carry):
            i = lax.rem(col + k, cols)
            mine = jnp.logical_and(on_diag, i == col)
            body(i, mine)
            return carry

        lax.fori_loop(0, cols, step, 0)

    plane(lambda to: pl.semaphore_signal(barrier, inc=1, device_id=(to, col), device_id_type=MESH))

    def greet(i, mine):
        @pl.when(jnp.logical_not(mine))
        def _():
            pl.semaphore_signal(barrier, inc=1, device_id=dest(i), device_id_type=MESH)
            pl.semaphore_signal(barrier, inc=1, device_id=source(i), device_id_type=MESH)

    across(greet)

    r_id = lax.broadcasted_iota(jnp.int32, f_ref.shape[1:], 0)
    c_id = lax.broadcasted_iota(jnp.int32, f_ref.shape[1:], 1)
    below = (c_id < r_id).astype(jnp.float32)
    above = (c_id > r_id).astype(jnp.float32)

    def mask_block(b, carry):
        block = f_ref[b].astype(jnp.float32)
        d = flt[n_flt_diag + b]
        f2[b] = (block * (1.0 - d + d * below)).astype(jnp.bfloat16)
        f2[nrow * nslot + b] = (block * (1.0 - d + d * above)).astype(jnp.bfloat16)
        return carry

    n_flt_diag = ROUNDS * (2 * nrow + 2)
    lax.fori_loop(0, nrow * nslot, mask_block, 0)
    held[pl.ds(0, ncol)] = v0_ref[...]
    held[zero] = jnp.zeros(held.shape[1:], held.dtype)
    xs[...] = jnp.zeros_like(xs)

    n_in = jnp.where(on_diag, 2 * (cols - 1), 2 * cols) + rows - 1
    pl.semaphore_wait(barrier, n_in)

    def reduce_round(n, with_own):
        for i in range(nrow):
            acc = None
            sel = tbl[n_tbl + n * nrow + i] * (nrow * nslot)
            for s in range(nslot):
                b = i * nslot + s
                term = lax.dot_general(
                    held[tbl[n * (nrow * nslot) + b]], f2[sel + b], NT,
                    preferred_element_type=jnp.float32,
                )
                acc = term if acc is None else acc + term
            if with_own:
                at = n * ncol + row // cols + per * i
                cl = flt[(n * nrow + i) * 2]
                cu = flt[(n * nrow + i) * 2 + 1]
                acc = acc + (cl + cu * piv_ref[pl.ds(i, 1), :]) * held[at].astype(jnp.float32)
            psend[n, i] = acc

            mine = jnp.logical_and(on_diag, col == i)

            @pl.when(jnp.logical_not(mine))
            def _():
                pltpu.make_async_remote_copy(
                    src_ref=psend.at[n, i], dst_ref=precv.at[n, col],
                    send_sem=send1.at[n], recv_sem=recv1.at[n],
                    device_id=dest(i), device_id_type=MESH,
                ).start()

            @pl.when(mine)
            def _():
                precv[n, col] = acc

        @pl.when(on_diag)
        def _():
            pltpu.make_async_copy(
                precv.at[n, pl.ds(0, cols - 1)], precv.at[n, pl.ds(0, cols - 1)], recv1.at[n]
            ).wait()

        @pl.when(jnp.logical_not(on_diag))
        def _():
            pltpu.make_async_copy(precv.at[n], precv.at[n], recv1.at[n]).wait()

        total = precv[n, 0]
        for c in range(1, cols):
            total = total + precv[n, c]
        return total

    def spread(n, value):
        land[n, own_pos] = value.astype(jnp.bfloat16)

        def send(to):
            pltpu.make_async_remote_copy(
                src_ref=land.at[n, own_pos], dst_ref=land.at[n, own_pos],
                send_sem=send2.at[n], recv_sem=recv2.at[n],
                device_id=(to, col), device_id_type=MESH,
            ).start()

        plane(send)
        some = land.at[n, pl.ds(0, rows - 1)]
        pltpu.make_async_copy(some, some, recv2.at[n]).wait()
        held[pl.ds((n + 1) * ncol, ncol)] = land[n]

    n_own = ROUNDS * 2 * nrow

    def solve(n):
        y = reduce_round(n, True)
        xs[0] += flt[n_own + 2 * n] * y
        xs[1] += flt[n_own + 2 * n + 1] * y
        return y

    def level(t, carry):
        n = 2 * t
        spread(n, solve(n))
        w = reduce_round(n + 1, False)
        v = flt[n_own + 2 * n + 2] * own_ref[0] + flt[n_own + 2 * n + 3] * own_ref[1] - w
        spread(n + 1, v)
        return carry

    lax.fori_loop(0, LEVELS - 1, level, 0)
    solve(ROUNDS - 1)

    place = row % cols

    def give(c, mine):
        @pl.when(jnp.logical_not(mine))
        def _():
            pltpu.make_async_remote_copy(
                src_ref=xs, dst_ref=xrecv.at[place], send_sem=send3, recv_sem=recv3,
                device_id=source(c), device_id_type=MESH,
            ).start()

        @pl.when(mine)
        def _():
            xrecv[place] = xs[...]

    across(give)

    def drain(n, carry):
        @pl.when(on_diag)
        def _():
            part = psend.at[n, pl.ds(0, cols - 1)]
            pltpu.make_async_copy(part, part, send1.at[n]).wait()

        @pl.when(jnp.logical_not(on_diag))
        def _():
            pltpu.make_async_copy(psend.at[n], psend.at[n], send1.at[n]).wait()

        return carry

    lax.fori_loop(0, ROUNDS, drain, 0)

    def drain2(n, carry):
        some = land.at[n, pl.ds(0, rows - 1)]
        pltpu.make_async_copy(some, some, send2.at[n]).wait()
        return carry

    lax.fori_loop(0, ROUNDS - 1, drain2, 0)

    @pl.when(on_diag)
    def _():
        part = xrecv.at[pl.ds(0, cols - 1)]
        pltpu.make_async_copy(part, part, recv3).wait()
        pltpu.make_async_copy(part, part, send3).wait()

    @pl.when(jnp.logical_not(on_diag))
    def _():
        pltpu.make_async_copy(xrecv, xrecv, recv3).wait()
        pltpu.make_async_copy(xrecv, xrecv, send3).wait()

    for i in range(nrow):
        low_ref[:, i, :] = xrecv[i, 0]
        up_ref[:, i, :] = xrecv[i, 1]


def shards(factor, inverse_pivot, lower_rhs, upper_rhs, snode_of_block, level_of_snode, slot_columns):
    rows, cols = lax.axis_size("row"), lax.axis_size("col")
    row, col = lax.axis_index("row"), lax.axis_index("col")
    nrow, nslot, size = factor.shape[:3]
    nrhs, ncol = lower_rhs.shape[:2]
    total = snode_of_block.shape[0]
    i32, f32 = jnp.int32, jnp.float32
    zero = ROUNDS * ncol

    ids = jnp.arange(total, dtype=i32)
    hot = snode_of_block[:, None] == jnp.arange(level_of_snode.shape[0], dtype=i32)[None, :]
    levels = jnp.sum(jnp.where(hot, level_of_snode[None, :], 0), axis=1)

    def look(table, at):
        return jnp.sum(jnp.where(at[..., None] == ids, table, 0), axis=-1)

    row_ids = jnp.arange(nrow, dtype=i32) * rows + row
    col_ids = jnp.arange(ncol, dtype=i32) * cols + col
    own_id = (row // cols) * cols + col + rows * (row % cols)
    row_level, row_snode = look(levels, row_ids), look(snode_of_block, row_ids)
    col_level, own_level = look(levels, col_ids), look(levels, own_id)
    slot_level, slot_snode = look(levels, slot_columns), look(snode_of_block, slot_columns)
    valid = slot_columns < total
    same = valid & (slot_snode == row_snode[:, None])
    other = valid & (slot_snode != row_snode[:, None])
    diag = slot_columns == row_ids[:, None]
    place = slot_columns // cols
    lo_in = (same & (slot_columns < row_ids[:, None])) | diag
    up_in = (same & (slot_columns > row_ids[:, None])) | diag
    lo_out = other & (row_level[:, None] > slot_level)
    up_out = other & (row_level[:, None] < slot_level)
    top = LEVELS - 1

    n = jnp.arange(ROUNDS, dtype=i32)
    t = n // 2
    inside = (n % 2 == 0)[:, None, None]
    at = (t + n % 2)[:, None]
    is_lo, is_up = row_level[None] == at, row_level[None] == top - at
    in_pick = n[:, None, None] * ncol + place[None]
    lo_pick = jnp.where(inside, in_pick, (2 * slot_level[None] + 1) * ncol + place[None])
    up_pick = jnp.where(inside, in_pick, (2 * (top - slot_level[None]) + 1) * ncol + place[None])
    lo_on = is_lo[:, :, None] & jnp.where(inside, lo_in[None], lo_out[None])
    up_on = is_up[:, :, None] & jnp.where(inside, up_in[None], up_out[None])
    picks = jnp.where(lo_on, lo_pick, jnp.where(up_on, up_pick, zero))
    tbl = jnp.concatenate([picks.reshape(-1), is_up.astype(i32).reshape(-1)])

    on_diag = row % cols == col
    own_w = jnp.stack([is_lo & on_diag, is_up & on_diag], axis=-1).astype(f32)
    mine = jnp.stack([own_level == at[:, 0], own_level == top - at[:, 0]], axis=-1).astype(f32)
    flt = jnp.concatenate([own_w.reshape(-1), mine.reshape(-1), diag.astype(f32).reshape(-1)])

    first = jnp.where((col_level == 0)[None, :, None], lower_rhs, 0.0) + jnp.where(
        (col_level == top)[None, :, None], upper_rhs, 0.0
    )
    v0 = jnp.transpose(first.astype(jnp.bfloat16), (1, 0, 2))
    own_pos = row // cols + (rows // cols) * (row % cols)
    own = jnp.stack([
        lax.dynamic_index_in_dim(lower_rhs, own_pos, 1, keepdims=False),
        lax.dynamic_index_in_dim(upper_rhs, own_pos, 1, keepdims=False),
    ])

    vmem, smem = pl.BlockSpec(memory_space=pltpu.VMEM), pl.BlockSpec(memory_space=pltpu.SMEM)
    dma = pltpu.SemaphoreType.DMA
    blocks = nrow * nslot
    return pl.pallas_call(
        functools.partial(kernel, (rows, cols, nrow, nslot, ncol)),
        out_shape=[jax.ShapeDtypeStruct((nrhs, nrow, size), f32)] * 2,
        in_specs=[smem, smem, vmem, vmem, vmem, vmem],
        out_specs=[vmem, vmem],
        scratch_shapes=[
            pltpu.VMEM((2 * blocks, size, size), jnp.bfloat16),
            pltpu.VMEM((zero + 1, nrhs, size), jnp.bfloat16),
            pltpu.VMEM((ROUNDS - 1, ncol, nrhs, size), jnp.bfloat16),
            pltpu.VMEM((ROUNDS, nrow, nrhs, size), f32),
            pltpu.VMEM((ROUNDS, cols, nrhs, size), f32),
            pltpu.VMEM((2, nrhs, size), f32),
            pltpu.VMEM((nrow, 2, nrhs, size), f32),
            dma((ROUNDS,)), dma((ROUNDS,)), dma((ROUNDS - 1,)), dma((ROUNDS - 1,)), dma, dma,
        ],
        compiler_params=pltpu.CompilerParams(
            collective_id=0, has_side_effects=True, vmem_limit_bytes=32 * 2**20
        ),
        cost_estimate=pl.CostEstimate(
            flops=2 * ROUNDS * blocks * size * size * nrhs,
            bytes_accessed=4 * blocks * size * size, transcendentals=0,
        ),
    )(tbl, flt, factor.reshape(blocks, size, size), v0, own, inverse_pivot)


def solution(mesh):
    in_specs = (
        P("row", "col", None, None),
        P("row", None),
        P(None, "col", None),
        P(None, "col", None),
        P(),
        P(),
        P("row", "col"),
    )
    out_specs = (P(None, "row", None), P(None, "row", None))
    return jax.shard_map(shards, mesh=mesh, in_specs=in_specs, out_specs=out_specs, check_vma=False)
```

time: 778 us -> 164 us (0.21); the launches traced: 764 us -> 164 us
  blocking collectives: 529 us -> 0 us
  local copies, waits for them, and re-layouts: 160 us -> 3.66 us
  Pallas kernels: 0 us -> 151 us
  other arithmetic: 42.1 us -> 8.16 us
  matrix products: 12.2 us -> 0 us
  starting transfers between devices: 9.02 us -> 0 us
    all_gather x11 -> x0, blocking collectives: 275 us -> none  [the longest x10 256 us: in_one_piece(): lax.all_gather(both, axis, axis=dim, tiled=True)]
    all_to_all x20 -> x0, blocking collectives: 254 us -> none  [the longest x10 148 us: in_one_piece_2(): lax.all_to_all(both, axis, split_axis=split_dim, concat_axis=concat_dim,...]
    pallas_call x0 -> x1, Pallas kernels: none -> 151 us  [shards(): pl.pallas_call(functools.partial(kernel, (rows, cols, nrow, nslot, ncol))...]
    convert_element_type x30 -> x3, local copies, waits for them, and re-layouts: 56 us -> 0.32 us  [the longest x1 0.15 us: shards(): own_w = jnp.stack([is_lo & on_diag, is_up & on_diag], axis=-1).astype(f32)]
    unnamed x315 -> x6, local copies, waits for them, and re-layouts: 47.7 us -> 1.27 us
    gather x29 -> x0, local copies, waits for them, and re-layouts: 17.3 us -> none  [the longest x22 13 us: picked(): taken = jnp.take(values, local_cols, axis=1)]
    split x25 -> x0, local copies, waits for them, and re-layouts: 15.5 us -> none  [the longest x15 10.7 us: in_one_piece_2(): jnp.split(lax.all_to_all(both, axis, split_axis=split_dim, concat_axis=co...]
    convert_element_type x27 -> x0, other arithmetic: 14.9 us -> none  [the longest x5 9.4 us: shards(): lower_res = lower_res - lower_moved.astype(jnp.float32)]
  transfers between devices with their start and end apart: 1 -> 0, of which waited for: 1 -> 0; matrix products, arithmetic and copies ran while one was open for 0% -> 0% of each run, Pallas kernels for 0% -> 0%
where the time goes in v1:
time: 164 us
  Pallas kernels  151 us (92%)
  other arithmetic  8.16 us (5%)
  local copies, waits for them, and re-layouts  3.66 us (2%)
    pallas_call x1, Pallas kernels, shards(): pl.pallas_call(functools.partial(kernel, (rows, cols, nrow, nslot, ncol))...  151 us

profile of v1, /device:TPU:1, one launch (start us, length us, event | category | flops | bytes accessed | tf_op | source)
XLA Modules:
  0.0 164.0 jit_solution(12069219952157557703)
XLA Ops:
  0.7 0.9 select_reduce_fusion
  1.6 0.6 fusion.7
  2.2 0.2 select_reduce_fusion.1
  2.4 0.7 subtract_compare_fusion
  3.1 0.9 select_reduce_fusion.4
  4.0 0.1 copy.52
  4.3 1.0 select_reduce_fusion.3
  5.3 0.7 and_or_fusion.1
  6.0 0.7 compare_and_fusion.3
  6.7 0.1 copy.45
  6.8 0.1 copy.49
  6.9 0.1 copy.44
  7.0 0.1 copy.48
  7.1 0.1 copy.53
  7.2 0.7 multiply_add_fusion.1
  8.2 0.2 copy.51
  8.3 0.1 convert_element_type.23
  8.7 0.9 constant_dynamic-slice_fusion
  9.6 0.1 fusion.3
  9.8 0.1 reshape.307
  9.9 1.4 fusion.2.v0_ref
  11.3 151.4 %shard_map.86 = (f32[16,8,128]{2,1,0:T(8,128)S(1)}, f32[16,8,128]{2,1,0:T(8,128)S(1)}) custom-call(s32[440]{0:T(512)S(1)} %pad_add_fusion.1.tbl, f32[230]{0:T(256)S(1)} %add_convert_fusion.flt, bf16[32,128,128]{2,1,0:T(8,128)(2,1)S(1)} %bitcast.5, bf16[32,16,128]{2,1,0:T(8,128)(2,1)S(1)} %fusion.2.v0_ref, f32[2,16,128]{2,1,0:T(8,128)S(1)} %pad_maximum_fusion.own_ref, ...), custom_call_target="tpu_custom_call" | custom-call | flops 184549376 | bytes 2097152 | tf_op jit(solution)/shard_map/pallas_call | solution.py:282
  162.7 0.6 copy.70
  163.4 0.6 copy.71
  (25 shorter events, 0.9 us)
Async XLA Ops:
  0.6 10.7 %copy-start = (bf16[8,4,128,128]{3,2,1,0:T(8,128)(2,1)S(1)}, bf16[8,4,128,128]{3,2,1,0:T(8,128)(2,1)}, u32[]{:S(2)}) copy-start(bf16[8,4,128,128]{3,2,1,0:T(8,128)(2,1)} %param.7) | copy-start | bytes 3145732
  9.9 1.4 copy-start.1

commit v2 on v1

v2 whole, which is shorter than its diff:
```python
import functools

import jax
import jax.numpy as jnp
from jax import lax
from jax.experimental import pallas as pl
from jax.experimental.pallas import tpu as pltpu
from jax.sharding import PartitionSpec as P

MESH = pl.DeviceIdType.MESH
LEVELS = 6
TOP = LEVELS - 1
ROUNDS = 2 * LEVELS - 1
NT = (((1,), (1,)), ((), ()))
SIDE, CORES = 4, 2
FAR = 4096


def ring(d, n):
    return min(d % n, -d % n)


PLANE = sorted(
    [(a, b, c) for a in range(SIDE) for b in range(SIDE) for c in range(CORES)],
    key=lambda o: (-ring(o[0], SIDE) - ring(o[1], SIDE), -o[2]),
)
LINE = [o for o in PLANE if o[0] == 0]


def kernel(
    dims, snode, level, slots, f_hbm, low_hbm, up_hbm, piv_hbm, low_ref, up_ref,
    tbl, rlev, f_ref, low, up, piv, f2, held, land, psend, precv, xs, xrecv, last, zrecv,
    sem_in, send1, recv1, send2, recv2, send3, recv3, send4, recv4,
):
    rows, cols, nrow, nslot, ncol = dims
    nrhs = held.shape[1]
    per = rows // cols
    blocks = nrow * nslot
    total_blocks = rows * nrow
    zero = ROUNDS * ncol
    row, col = lax.axis_index("row"), lax.axis_index("col")
    y, x, core = row // (SIDE * CORES), row // CORES % SIDE, row % CORES
    base, lane = (row // cols) * cols, row % cols
    on_diag = col == lane
    off_diag = jnp.logical_not(on_diag)
    own_pos = row // cols + per * lane
    ys = [lax.rem(y + d, SIDE) * (SIDE * CORES) for d in range(SIDE)]
    xc = [[lax.rem(x + d, SIDE) * CORES + lax.rem(core + e, CORES) for e in range(CORES)] for d in range(SIDE)]
    zs = sorted(range(1, cols), key=lambda d: -ring(d, cols))

    copies = [
        pltpu.make_async_copy(src, dst, sem_in.at[k])
        for k, (src, dst) in enumerate([(low_hbm, low), (up_hbm, up), (f_hbm, f_ref), (piv_hbm, piv)])
    ]
    for copy in copies:
        copy.start()

    barrier = pltpu.get_barrier_semaphore()

    def greet(to):
        pl.semaphore_signal(barrier, inc=1, device_id=to, device_id_type=MESH)

    for dy, dx, dc in PLANE[:-1]:
        greet((ys[dy] + xc[dx][dc], col))
    for d in zs:
        greet((row, lax.rem(col + d, cols)))
    for _, dx, dc in LINE[:-1]:
        greet((base + xc[dx][dc], lane))
    for d in zs:
        greet((base + col, lax.rem(col + d, cols)))

    @pl.when(off_diag)
    def _():
        greet((base + lane, lane))
        greet((base + col, col))

    for i in range(nrow):
        rlev[i] = level[snode[row + rows * i]]

    own_level = level[snode[base + col + rows * lane]]

    def slot(b, carry):
        i = b // nslot
        this = row + rows * i
        lev, sn = rlev[i], snode[this]
        j = slots[b]
        valid = j < total_blocks
        jj = jnp.minimum(j, total_blocks - 1)
        j_sn = snode[jj]
        j_lev = level[j_sn]
        same = valid & (j_sn == sn)
        other = valid & (j_sn != sn)
        place = jj // cols
        lo_in = jnp.where((same & (j < this)) | (j == this), place, FAR)
        up_in = jnp.where((same & (j > this)) | (j == this), place, FAR)
        lo_out = jnp.where(other & (lev > j_lev), (2 * j_lev + 1) * ncol + place, zero)
        up_out = jnp.where(other & (lev < j_lev), (2 * (TOP - j_lev) + 1) * ncol + place, zero)
        for t in range(LEVELS):
            pick = jnp.where(lev == t, lo_in, jnp.where(lev == TOP - t, up_in, FAR))
            tbl[2 * t * blocks + b] = jnp.minimum(pick + 2 * t * ncol, zero)
            if t < TOP:
                pick = jnp.where(lev == t + 1, lo_out, jnp.where(lev == TOP - 1 - t, up_out, zero))
                tbl[(2 * t + 1) * blocks + b] = pick
        return carry

    lax.fori_loop(0, blocks, slot, 0)

    def one(flag):
        return jnp.where(flag, 1.0, 0.0).astype(jnp.float32)

    copies[0].wait()
    copies[1].wait()
    for j in range(ncol):
        lev = level[snode[j * cols + col]]
        rows_of = pl.ds(j, nrhs, stride=ncol)
        held[j] = (one(lev == 0) * low[rows_of, :] + one(lev == TOP) * up[rows_of, :]).astype(jnp.bfloat16)
    held[zero] = jnp.zeros(held.shape[1:], held.dtype)
    xs[...] = jnp.zeros_like(xs)
    mine_rows = pl.ds(own_pos, nrhs, stride=ncol)

    r_id = lax.broadcasted_iota(jnp.int32, f_ref.shape[1:], 0)
    c_id = lax.broadcasted_iota(jnp.int32, f_ref.shape[1:], 1)
    below = (c_id < r_id).astype(jnp.float32)
    above = (c_id > r_id).astype(jnp.float32)
    copies[2].wait()
    copies[3].wait()

    def mask_block(b, carry):
        block = f_ref[b].astype(jnp.float32)
        d = one(slots[b] == row + rows * (b // nslot))
        f2[b] = (block * (1.0 - d + d * below)).astype(jnp.bfloat16)
        f2[blocks + b] = (block * (1.0 - d + d * above)).astype(jnp.bfloat16)
        return carry

    lax.fori_loop(0, blocks, mask_block, 0)

    def row_sum(n, i, t):
        acc = None
        lev = rlev[i]
        sel = 0
        if t is not None:
            sel = jnp.where(lev == TOP - t, blocks, 0)
        for s in range(nslot):
            b = i * nslot + s
            term = lax.dot_general(
                held[tbl[n * blocks + b]], f2[sel + b], NT, preferred_element_type=jnp.float32
            )
            acc = term if acc is None else acc + term
        if t is not None:
            own = held[n * ncol + row // cols + per * i].astype(jnp.float32)
            w = one(on_diag & (lev == t)) + one(on_diag & (lev == TOP - t)) * piv[pl.ds(i, 1), :]
            acc = acc + w * own
        return acc

    def part_copy(n, i, dx, dc):
        return pltpu.make_async_remote_copy(
            src_ref=psend.at[n, i], dst_ref=precv.at[n, col], send_sem=send1.at[n], recv_sem=recv1.at[n],
            device_id=(base + i, lane), device_id_type=MESH,
        )

    def parts(n, t, wait_first):
        if wait_first:
            for _, dx, dc in LINE:
                i = xc[dx][dc]
                psend[n, i] = row_sum(n, i, t).astype(jnp.bfloat16)
            wait_first()
        for _, dx, dc in LINE:
            i = xc[dx][dc]
            if not wait_first:
                psend[n, i] = row_sum(n, i, t).astype(jnp.bfloat16)
            if dx or dc:
                part_copy(n, i, dx, dc).start()
            else:
                @pl.when(off_diag)
                def _():
                    part_copy(n, i, dx, dc).start()

                @pl.when(on_diag)
                def _():
                    precv[n, col] = psend[n, i]

    def wait_bytes(ref, count, sem):
        @pl.when(on_diag)
        def _():
            part = ref.at[pl.ds(0, count - 1)]
            pltpu.make_async_copy(part, part, sem).wait()

        @pl.when(off_diag)
        def _():
            part = ref.at[pl.ds(0, count)]
            pltpu.make_async_copy(part, part, sem).wait()

    def gathered(n):
        wait_bytes(precv.at[n], cols, recv1.at[n])
        return jnp.sum(precv[n].astype(jnp.float32), axis=0)

    def spread(n, value):
        land[n, own_pos] = value.astype(jnp.bfloat16)
        mine = land.at[n, own_pos]
        for dy, dx, dc in PLANE[:-1]:
            pltpu.make_async_remote_copy(
                src_ref=mine, dst_ref=mine, send_sem=send2.at[n], recv_sem=recv2.at[n],
                device_id=(ys[dy] + xc[dx][dc], col), device_id_type=MESH,
            ).start()

    def spread_wait(n):
        some = land.at[n, pl.ds(0, rows - 1)]
        pltpu.make_async_copy(some, some, recv2.at[n]).wait()
        held[pl.ds((n + 1) * ncol, ncol)] = land[n]

    def give_copy(d):
        return pltpu.make_async_remote_copy(
            src_ref=xs, dst_ref=xrecv.at[lane], send_sem=send3, recv_sem=recv3,
            device_id=(base + col, lax.rem(col + d, cols)), device_id_type=MESH,
        )

    def give():
        for d in zs:
            give_copy(d).start()

        @pl.when(off_diag)
        def _():
            give_copy(0).start()

        @pl.when(on_diag)
        def _():
            xrecv[lane] = xs[...]

    n_in = jnp.where(on_diag, 2 * (cols - 1), 2 * cols) + rows - 1 + cols - 1

    def level_step(t, first):
        n = 2 * t
        parts(n, t, first)
        sol = gathered(n)
        spread(n, sol)
        xs[0] += one(own_level == t) * sol
        xs[1] += one(own_level == TOP - t) * sol

        @pl.when(t == TOP - 1)
        def _():
            give()

        spread_wait(n)
        parts(n + 1, None, None)
        w = gathered(n + 1)
        rhs = one(own_level == t + 1) * low[mine_rows, :] + one(own_level == TOP - 1 - t) * up[mine_rows, :]
        spread(n + 1, rhs - w)
        spread_wait(n + 1)

    level_step(0, lambda: pl.semaphore_wait(barrier, n_in))

    def body(t, carry):
        level_step(t, None)
        return carry

    lax.fori_loop(1, TOP, body, 0)

    n = ROUNDS - 1
    for i in range(nrow):
        last[i] = row_sum(n, i, TOP).astype(jnp.bfloat16)
    zrecv[col] = last[...]
    for d in zs:
        pltpu.make_async_remote_copy(
            src_ref=last, dst_ref=zrecv.at[col], send_sem=send4, recv_sem=recv4,
            device_id=(row, lax.rem(col + d, cols)), device_id_type=MESH,
        ).start()

    def drain(m, carry):
        wait_bytes(psend.at[m], cols, send1.at[m])
        some = land.at[m, pl.ds(0, rows - 1)]
        pltpu.make_async_copy(some, some, send2.at[m]).wait()
        return carry

    lax.fori_loop(0, ROUNDS - 1, drain, 0)
    wait_bytes(xrecv, cols, recv3)
    wait_bytes(xrecv, cols, send3)
    some = zrecv.at[pl.ds(0, cols - 1)]
    pltpu.make_async_copy(some, some, recv4).wait()
    for i in range(nrow):
        sol = jnp.sum(zrecv[:, i].astype(jnp.float32), axis=0)
        lev = rlev[i]
        low_ref[:, i, :] = xrecv[i, 0] + one(lev == TOP) * sol
        up_ref[:, i, :] = xrecv[i, 1] + one(lev == 0) * sol
    pltpu.make_async_copy(some, some, send4).wait()


def shards(factor, inverse_pivot, lower_rhs, upper_rhs, snode_of_block, level_of_snode, slot_columns):
    rows, cols = lax.axis_size("row"), lax.axis_size("col")
    nrow, nslot, size = factor.shape[:3]
    nrhs, ncol = lower_rhs.shape[:2]
    f32, bf16 = jnp.float32, jnp.bfloat16
    blocks = nrow * nslot
    vmem, smem = pl.BlockSpec(memory_space=pltpu.VMEM), pl.BlockSpec(memory_space=pltpu.SMEM)
    hbm = pl.BlockSpec(memory_space=pl.ANY)
    dma = pltpu.SemaphoreType.DMA
    return pl.pallas_call(
        functools.partial(kernel, (rows, cols, nrow, nslot, ncol)),
        out_shape=[jax.ShapeDtypeStruct((nrhs, nrow, size), f32)] * 2,
        in_specs=[smem, smem, smem, hbm, hbm, hbm, hbm],
        out_specs=[vmem, vmem],
        scratch_shapes=[
            pltpu.SMEM((ROUNDS * blocks,), jnp.int32),
            pltpu.SMEM((nrow,), jnp.int32),
            pltpu.VMEM((blocks, size, size), bf16),
            pltpu.VMEM((nrhs * ncol, size), f32),
            pltpu.VMEM((nrhs * ncol, size), f32),
            pltpu.VMEM((nrow, size), f32),
            pltpu.VMEM((2 * blocks, size, size), bf16),
            pltpu.VMEM((ROUNDS * ncol + 1, nrhs, size), bf16),
            pltpu.VMEM((ROUNDS - 1, ncol, nrhs, size), bf16),
            pltpu.VMEM((ROUNDS - 1, nrow, nrhs, size), bf16),
            pltpu.VMEM((ROUNDS - 1, cols, nrhs, size), bf16),
            pltpu.VMEM((2, nrhs, size), f32),
            pltpu.VMEM((nrow, 2, nrhs, size), f32),
            pltpu.VMEM((nrow, nrhs, size), bf16),
            pltpu.VMEM((cols, nrow, nrhs, size), bf16),
            dma((4,)),
            dma((ROUNDS - 1,)), dma((ROUNDS - 1,)), dma((ROUNDS - 1,)), dma((ROUNDS - 1,)),
            dma, dma, dma, dma,
        ],
        compiler_params=pltpu.CompilerParams(
            collective_id=0, has_side_effects=True, vmem_limit_bytes=32 * 2**20
        ),
        cost_estimate=pl.CostEstimate(
            flops=2 * ROUNDS * blocks * size * size * nrhs,
            bytes_accessed=4 * blocks * size * size, transcendentals=0,
        ),
    )(
        snode_of_block, level_of_snode, slot_columns.reshape(-1),
        factor.reshape(blocks, size, size), lower_rhs.reshape(nrhs * ncol, size),
        upper_rhs.reshape(nrhs * ncol, size), inverse_pivot,
    )


def solution(mesh):
    in_specs = (
        P("row", "col", None, None),
        P("row", None),
        P(None, "col", None),
        P(None, "col", None),
        P(),
        P(),
        P("row", "col"),
    )
    out_specs = (P(None, "row", None), P(None, "row", None))
    return jax.shard_map(shards, mesh=mesh, in_specs=in_specs, out_specs=out_specs, check_vma=False)
```

time: 164 us -> 139 us (0.85)
  Pallas kernels: 151 us -> 132 us
  other arithmetic: 8.16 us -> 0 us
  local copies, waits for them, and re-layouts: 3.66 us -> 5.82 us
    pallas_call x1, Pallas kernels: 151 us -> 132 us  [shards(): pl.pallas_call(functools.partial(kernel, (rows, cols, nrow, nslot, ncol))...]
    unnamed x6 -> x17, local copies, waits for them, and re-layouts: 1.27 us -> 5.74 us
    reduce_sum x5 -> x0, other arithmetic: 3.55 us -> none  [the longest x4 2.69 us: look(): return jnp.sum(jnp.where(at[..., None] == ids, table, 0), axis=-1)]
where the time goes in v2:
time: 139 us; the launch traced here: 138 us
  Pallas kernels  132 us (95%)
  local copies, waits for them, and re-layouts  5.82 us (4%)
    pallas_call x1, Pallas kernels, shards(): pl.pallas_call(functools.partial(kernel, (rows, cols, nrow, nslot, ncol))...  132 us
    unnamed x17, local copies, waits for them, and re-layouts  5.74 us

profile of v2, /device:TPU:1, one launch (start us, length us, event | category | flops | bytes accessed | tf_op | source)
XLA Modules:
  0.0 138.3 jit_solution(10763266775379812758)
XLA Ops:
  0.6 0.0 copy-start.6
  0.6 0.7 copy-done.6
  1.3 0.0 copy-start.3
  1.3 0.1 copy.10
  1.4 0.0 copy-start.4
  1.4 0.0 copy-start.5
  1.4 0.1 reshape.16.slots
  1.5 0.5 copy-done.3
  2.0 0.1 copy-done.4
  2.1 0.0 copy-done.5
  2.1 0.0 copy-start
  2.1 1.2 copy-done
  3.3 0.0 copy-start.1
  3.3 0.9 copy-done.1
  4.3 0.0 copy-start.2
  4.3 0.9 copy-done.2
  5.2 131.8 %shard_map.86 = (f32[16,8,128]{2,1,0:T(8,128)S(1)}, f32[16,8,128]{2,1,0:T(8,128)S(1)}) custom-call(s32[256]{0:T(256)S(1)} %copy-done.4, s32[64]{0:T(128)S(1)} %copy-done.5, s32[32]{0:T(128)S(1)} %reshape.16.slots, bf16[32,128,128]{2,1,0:T(8,128)(2,1)S(1)} %bitcast.3, f32[512,128]{1,0:T(8,128)S(1)} %bitcast.4, f32[512,128]{1,0:T(8,128)S(1)} %bitcast.5, ...), custom_call_target="tpu_custom_call" | custom-call | flops 184549376 | bytes 2097152 | tf_op jit(solution)/shard_map/pallas_call | solution.py:296
  137.0 0.6 copy.13
  137.7 0.6 copy.14
Async XLA Ops:
  0.6 0.7 copy-start.6
  1.3 0.7 copy-start.3
  1.4 0.7 copy-start.4
  1.4 0.7 copy-start.5
  2.1 1.2 copy-start
  3.3 0.9 copy-start.1
  4.3 0.9 copy-start.2

commit v3 on v2

--- a/solution.py
+++ b/solution.py
@@ -11,9 +11,9 @@
 LEVELS = 6
 TOP = LEVELS - 1
 ROUNDS = 2 * LEVELS - 1
-NT = (((1,), (1,)), ((), ()))
 SIDE, CORES = 4, 2
 FAR = 4096
+VMEM_MIB = 60
 
 
 def ring(d, n):
@@ -29,8 +29,8 @@
 
 def kernel(
     dims, snode, level, slots, f_hbm, low_hbm, up_hbm, piv_hbm, low_ref, up_ref,
-    tbl, rlev, f_ref, low, up, piv, f2, held, land, psend, precv, xs, xrecv, last, zrecv,
-    sem_in, send1, recv1, send2, recv2, send3, recv3, send4, recv4,
+    tbl, rlev, f_ref, low, up, piv, f2, piv8, own_piv, held, land, psend, precv, xs, xrecv, last, zrecv,
+    sem_in, send1, recv1, send2, recv2, send3, recv3, send4, recv4, send5, recv5,
 ):
     rows, cols, nrow, nslot, ncol = dims
     nrhs = held.shape[1]
@@ -50,7 +50,7 @@
 
     copies = [
         pltpu.make_async_copy(src, dst, sem_in.at[k])
-        for k, (src, dst) in enumerate([(low_hbm, low), (up_hbm, up), (f_hbm, f_ref), (piv_hbm, piv)])
+        for k, (src, dst) in enumerate([(f_hbm, f_ref), (low_hbm, low), (up_hbm, up), (piv_hbm, piv)])
     ]
     for copy in copies:
         copy.start()
@@ -59,20 +59,21 @@
 
     def greet(to):
         pl.semaphore_signal(barrier, inc=1, device_id=to, device_id_type=MESH)
+
+    for d in zs:
+        greet((base + col, lax.rem(col + d, cols)))
+    for _, dx, dc in LINE[:-1]:
+        greet((base + xc[dx][dc], lane))
+
+    @pl.when(off_diag)
+    def _():
+        greet((base + lane, lane))
+        greet((base + col, col))
 
     for dy, dx, dc in PLANE[:-1]:
         greet((ys[dy] + xc[dx][dc], col))
     for d in zs:
         greet((row, lax.rem(col + d, cols)))
-    for _, dx, dc in LINE[:-1]:
-        greet((base + xc[dx][dc], lane))
-    for d in zs:
-        greet((base + col, lax.rem(col + d, cols)))
-
-    @pl.when(off_diag)
-    def _():
-        greet((base + lane, lane))
-        greet((base + col, col))
 
     for i in range(nrow):
         rlev[i] = level[snode[row + rows * i]]
@@ -83,7 +84,7 @@
         i = b // nslot
         this = row + rows * i
         lev, sn = rlev[i], snode[this]
-        j = slots[b]
+        j = slots[b % nslot, i]
         valid = j < total_blocks
         jj = jnp.minimum(j, total_blocks - 1)
         j_sn = snode[jj]
@@ -108,8 +109,8 @@
     def one(flag):
         return jnp.where(flag, 1.0, 0.0).astype(jnp.float32)
 
-    copies[0].wait()
     copies[1].wait()
+    copies[2].wait()
     for j in range(ncol):
         lev = level[snode[j * cols + col]]
         rows_of = pl.ds(j, nrhs, stride=ncol)
@@ -120,64 +121,49 @@
 
     r_id = lax.broadcasted_iota(jnp.int32, f_ref.shape[1:], 0)
     c_id = lax.broadcasted_iota(jnp.int32, f_ref.shape[1:], 1)
-    below = (c_id < r_id).astype(jnp.float32)
-    above = (c_id > r_id).astype(jnp.float32)
-    copies[2].wait()
+    below = jnp.where(r_id < c_id, 0.0, -1.0).astype(jnp.bfloat16)
+    above = jnp.where(r_id > c_id, 0.0, -1.0).astype(jnp.bfloat16)
+    copies[0].wait()
     copies[3].wait()
+    for i in range(nrow):
+        piv8[i] = jnp.broadcast_to(piv[i : i + 1, :], piv8.shape[1:])
 
     def mask_block(b, carry):
-        block = f_ref[b].astype(jnp.float32)
-        d = one(slots[b] == row + rows * (b // nslot))
-        f2[b] = (block * (1.0 - d + d * below)).astype(jnp.bfloat16)
-        f2[blocks + b] = (block * (1.0 - d + d * above)).astype(jnp.bfloat16)
+        block = f_ref[b].T
+        d = one(slots[b % nslot, b // nslot] == row + rows * (b // nslot)).astype(jnp.bfloat16)
+        i, at = b // nslot, pl.ds(pl.multiple_of(b % nslot * f_ref.shape[1], f_ref.shape[1]), f_ref.shape[1])
+        f2[i, at] = block + block * (d * below)
+        f2[nrow + i, at] = block + block * (d * above)
         return carry
 
-    lax.fori_loop(0, blocks, mask_block, 0)
+    lax.fori_loop(0, blocks, mask_block, 0, unroll=4)
 
     def row_sum(n, i, t):
-        acc = None
-        lev = rlev[i]
-        sel = 0
-        if t is not None:
-            sel = jnp.where(lev == TOP - t, blocks, 0)
-        for s in range(nslot):
-            b = i * nslot + s
-            term = lax.dot_general(
-                held[tbl[n * blocks + b]], f2[sel + b], NT, preferred_element_type=jnp.float32
-            )
-            acc = term if acc is None else acc + term
-        if t is not None:
-            own = held[n * ncol + row // cols + per * i].astype(jnp.float32)
-            w = one(on_diag & (lev == t)) + one(on_diag & (lev == TOP - t)) * piv[pl.ds(i, 1), :]
-            acc = acc + w * own
-        return acc
-
-    def part_copy(n, i, dx, dc):
+        side = i if t is None else i + jnp.where(rlev[i] == TOP - t, nrow, 0)
+        picked = [held[tbl[n * blocks + i * nslot + s]] for s in range(nslot)]
+        return jnp.dot(jnp.concatenate(picked, axis=1), f2[side], preferred_element_type=jnp.float32)
+
+    def part_copy(n, i):
         return pltpu.make_async_remote_copy(
             src_ref=psend.at[n, i], dst_ref=precv.at[n, col], send_sem=send1.at[n], recv_sem=recv1.at[n],
             device_id=(base + i, lane), device_id_type=MESH,
         )
 
-    def parts(n, t, wait_first):
-        if wait_first:
-            for _, dx, dc in LINE:
-                i = xc[dx][dc]
-                psend[n, i] = row_sum(n, i, t).astype(jnp.bfloat16)
-            wait_first()
-        for _, dx, dc in LINE:
-            i = xc[dx][dc]
-            if not wait_first:
-                psend[n, i] = row_sum(n, i, t).astype(jnp.bfloat16)
-            if dx or dc:
-                part_copy(n, i, dx, dc).start()
-            else:
-                @pl.when(off_diag)
-                def _():
-                    part_copy(n, i, dx, dc).start()
-
-                @pl.when(on_diag)
-                def _():
-                    precv[n, col] = psend[n, i]
+    def parts(n, t, ready):
+        sums = [row_sum(n, xc[dx][dc], t) for _, dx, dc in LINE]
+        for (_, dx, dc), value in zip(LINE, sums):
+            psend[n, xc[dx][dc]] = value.astype(jnp.bfloat16)
+        ready()
+        for _, dx, dc in LINE[:-1]:
+            part_copy(n, xc[dx][dc]).start()
+
+        @pl.when(off_diag)
+        def _():
+            part_copy(n, lane).start()
+
+        @pl.when(on_diag)
+        def _():
+            precv[n, col] = psend[n, col]
 
     def wait_bytes(ref, count, sem):
         @pl.when(on_diag)
@@ -226,12 +212,41 @@
         def _():
             xrecv[lane] = xs[...]
 
+    def piv_copy(to, i):
+        return pltpu.make_async_remote_copy(
+            src_ref=piv8.at[i], dst_ref=own_piv, send_sem=send5, recv_sem=recv5,
+            device_id=(base + to, lane), device_id_type=MESH,
+        )
+
+    def pivots_start():
+        @pl.when(on_diag)
+        def _():
+            for _, dx, dc in LINE[:-1]:
+                piv_copy(xc[dx][dc], xc[dx][dc]).start()
+            own_piv[...] = piv8[lane]
+
+    def pivots_wait():
+        @pl.when(on_diag)
+        def _():
+            some = piv8.at[pl.ds(0, cols - 1)]
+            pltpu.make_async_copy(some, some, send5).wait()
+
+        @pl.when(off_diag)
+        def _():
+            pltpu.make_async_copy(own_piv, own_piv, recv5).wait()
+
     n_in = jnp.where(on_diag, 2 * (cols - 1), 2 * cols) + rows - 1 + cols - 1
 
     def level_step(t, first):
         n = 2 * t
-        parts(n, t, first)
+        parts(n, t, lambda: pl.semaphore_wait(barrier, n_in) if first else None)
+        if first:
+            pivots_start()
         sol = gathered(n)
+        if first:
+            pivots_wait()
+        own = held[n * ncol + own_pos].astype(jnp.float32)
+        sol = sol + (one(own_level == t) + one(own_level == TOP - t) * own_piv[0:1, :]) * own
         spread(n, sol)
         xs[0] += one(own_level == t) * sol
         xs[1] += one(own_level == TOP - t) * sol
@@ -241,23 +256,25 @@
             give()
 
         spread_wait(n)
-        parts(n + 1, None, None)
+        parts(n + 1, None, lambda: None)
         w = gathered(n + 1)
         rhs = one(own_level == t + 1) * low[mine_rows, :] + one(own_level == TOP - 1 - t) * up[mine_rows, :]
         spread(n + 1, rhs - w)
         spread_wait(n + 1)
 
-    level_step(0, lambda: pl.semaphore_wait(barrier, n_in))
+    level_step(0, True)
 
     def body(t, carry):
-        level_step(t, None)
+        level_step(t, False)
         return carry
 
     lax.fori_loop(1, TOP, body, 0)
 
     n = ROUNDS - 1
     for i in range(nrow):
-        last[i] = row_sum(n, i, TOP).astype(jnp.bfloat16)
+        own = held[n * ncol + row // cols + per * i].astype(jnp.float32)
+        w = one(on_diag & (rlev[i] == TOP)) + one(on_diag & (rlev[i] == 0)) * piv8[i, 0:1, :]
+        last[i] = (row_sum(n, i, TOP) + w * own).astype(jnp.bfloat16)
     zrecv[col] = last[...]
     for d in zs:
         pltpu.make_async_remote_copy(
@@ -291,7 +308,7 @@
     f32, bf16 = jnp.float32, jnp.bfloat16
     blocks = nrow * nslot
     vmem, smem = pl.BlockSpec(memory_space=pltpu.VMEM), pl.BlockSpec(memory_space=pltpu.SMEM)
-    hbm = pl.BlockSpec(memory_space=pl.ANY)
+    hbm = pl.BlockSpec(memory_space=pltpu.HBM)
     dma = pltpu.SemaphoreType.DMA
     return pl.pallas_call(
         functools.partial(kernel, (rows, cols, nrow, nslot, ncol)),
@@ -305,7 +322,9 @@
             pltpu.VMEM((nrhs * ncol, size), f32),
             pltpu.VMEM((nrhs * ncol, size), f32),
             pltpu.VMEM((nrow, size), f32),
-            pltpu.VMEM((2 * blocks, size, size), bf16),
+            pltpu.VMEM((2 * nrow, nslot * size, size), bf16),
+            pltpu.VMEM((nrow, 8, size), f32),
+            pltpu.VMEM((8, size), f32),
             pltpu.VMEM((ROUNDS * ncol + 1, nrhs, size), bf16),
             pltpu.VMEM((ROUNDS - 1, ncol, nrhs, size), bf16),
             pltpu.VMEM((ROUNDS - 1, nrow, nrhs, size), bf16),
@@ -316,17 +335,17 @@
             pltpu.VMEM((cols, nrow, nrhs, size), bf16),
             dma((4,)),
             dma((ROUNDS - 1,)), dma((ROUNDS - 1,)), dma((ROUNDS - 1,)), dma((ROUNDS - 1,)),
-            dma, dma, dma, dma,
+            dma, dma, dma, dma, dma, dma,
         ],
         compiler_params=pltpu.CompilerParams(
-            collective_id=0, has_side_effects=True, vmem_limit_bytes=32 * 2**20
+            collective_id=0, has_side_effects=True, vmem_limit_bytes=VMEM_MIB * 2**20
         ),
         cost_estimate=pl.CostEstimate(
             flops=2 * ROUNDS * blocks * size * size * nrhs,
             bytes_accessed=4 * blocks * size * size, transcendentals=0,
         ),
     )(
-        snode_of_block, level_of_snode, slot_columns.reshape(-1),
+        snode_of_block, level_of_snode, slot_columns.T,
         factor.reshape(blocks, size, size), lower_rhs.reshape(nrhs * ncol, size),
         upper_rhs.reshape(nrhs * ncol, size), inverse_pivot,
     )

time: 139 us -> 127 us (0.914)
  Pallas kernels: 132 us -> 124 us
  local copies, waits for them, and re-layouts: 5.82 us -> 2.14 us
    pallas_call x1, Pallas kernels: 132 us -> 124 us  [shards(): pl.pallas_call(functools.partial(kernel, (rows, cols, nrow, nslot, ncol))...]
    unnamed x17 -> x4, local copies, waits for them, and re-layouts: 5.74 us -> 2.14 us
where the time goes in v3:
time: 127 us
  Pallas kernels  124 us (98%)
  local copies, waits for them, and re-layouts  2.14 us (2%)
    pallas_call x1, Pallas kernels, shards(): pl.pallas_call(functools.partial(kernel, (rows, cols, nrow, nslot, ncol))...  124 us

profile of v3, /device:TPU:1, one launch (start us, length us, event | category | flops | bytes accessed | tf_op | source)
XLA Modules:
  0.0 126.9 jit_solution(4097296541414550957)
XLA Ops:
  0.6 124.1 %shard_map.86 = (f32[16,8,128]{2,1,0:T(8,128)}, f32[16,8,128]{2,1,0:T(8,128)}) custom-call(s32[256]{0:T(256)} %snode.1, s32[64]{0:T(128)} %level.1, s32[4,8]{1,0:T(4,128)} %bitcast.7, bf16[32,128,128]{2,1,0:T(8,128)(2,1)} %bitcast.4, f32[512,128]{1,0:T(8,128)} %bitcast.5, f32[512,128]{1,0:T(8,128)} %bitcast.6, f32[8,128]{1,0:T(8,128)} %piv_hbm.1), custom_call_target="tpu_custom_call" | custom-call | flops 184549376 | bytes 2097152 | tf_op jit(solution)/shard_map/pallas_call | solution.py:313
  124.7 0.0 copy-start
  124.7 1.5 %copy.11 = f32[16,8,128]{2,1,0:T(8,128)} copy(f32[16,8,128]{2,1,0:T(8,128)} %get-tuple-element.4) | data formatting | bytes 131072
  126.2 0.0 copy-done
  126.2 0.6 copy.12
Async XLA Ops:
  124.7 1.5 %copy-start = (f32[16,8,128]{2,1,0:T(8,128)S(1)}, f32[16,8,128]{2,1,0:T(8,128)}, u32[]{:S(2)}) copy-start(f32[16,8,128]{2,1,0:T(8,128)} %get-tuple-element.5) | copy-start | bytes 196612

commit v4 on v3

--- a/solution.py
+++ b/solution.py
@@ -13,7 +13,7 @@
 ROUNDS = 2 * LEVELS - 1
 SIDE, CORES = 4, 2
 FAR = 4096
-VMEM_MIB = 60
+VMEM_MIB = 53.75
 
 
 def ring(d, n):
@@ -28,8 +28,8 @@
 
 
 def kernel(
-    dims, snode, level, slots, f_hbm, low_hbm, up_hbm, piv_hbm, low_ref, up_ref,
-    tbl, rlev, f_ref, low, up, piv, f2, piv8, own_piv, held, land, psend, precv, xs, xrecv, last, zrecv,
+    dims, snode_hbm, level_hbm, slots_hbm, f_hbm, low_hbm, up_hbm, piv_hbm, low_ref, up_ref,
+    snode, level, slots, tbl, rlev, f_ref, low, up, piv, f2, piv8, own_piv, held, land, psend, precv, xs, xrecv, last, zrecv,
     sem_in, send1, recv1, send2, recv2, send3, recv3, send4, recv4, send5, recv5,
 ):
     rows, cols, nrow, nslot, ncol = dims
@@ -50,7 +50,8 @@
 
     copies = [
         pltpu.make_async_copy(src, dst, sem_in.at[k])
-        for k, (src, dst) in enumerate([(f_hbm, f_ref), (low_hbm, low), (up_hbm, up), (piv_hbm, piv)])
+        for k, (src, dst) in enumerate([(f_hbm, f_ref), (low_hbm, low), (up_hbm, up), (piv_hbm, piv),
+            (snode_hbm, snode), (level_hbm, level), (slots_hbm, slots)])
     ]
     for copy in copies:
         copy.start()
@@ -75,6 +76,8 @@
     for d in zs:
         greet((row, lax.rem(col + d, cols)))
 
+    for copy in copies[4:]:
+        copy.wait()
     for i in range(nrow):
         rlev[i] = level[snode[row + rows * i]]
 
@@ -307,15 +310,18 @@
     nrhs, ncol = lower_rhs.shape[:2]
     f32, bf16 = jnp.float32, jnp.bfloat16
     blocks = nrow * nslot
-    vmem, smem = pl.BlockSpec(memory_space=pltpu.VMEM), pl.BlockSpec(memory_space=pltpu.SMEM)
+    vmem = pl.BlockSpec(memory_space=pltpu.VMEM)
     hbm = pl.BlockSpec(memory_space=pltpu.HBM)
     dma = pltpu.SemaphoreType.DMA
     return pl.pallas_call(
         functools.partial(kernel, (rows, cols, nrow, nslot, ncol)),
         out_shape=[jax.ShapeDtypeStruct((nrhs, nrow, size), f32)] * 2,
-        in_specs=[smem, smem, smem, hbm, hbm, hbm, hbm],
+        in_specs=[hbm] * 7,
         out_specs=[vmem, vmem],
         scratch_shapes=[
+            pltpu.SMEM(snode_of_block.shape, jnp.int32),
+            pltpu.SMEM(level_of_snode.shape, jnp.int32),
+            pltpu.SMEM((nslot, nrow), jnp.int32),
             pltpu.SMEM((ROUNDS * blocks,), jnp.int32),
             pltpu.SMEM((nrow,), jnp.int32),
             pltpu.VMEM((blocks, size, size), bf16),
@@ -333,12 +339,12 @@
             pltpu.VMEM((nrow, 2, nrhs, size), f32),
             pltpu.VMEM((nrow, nrhs, size), bf16),
             pltpu.VMEM((cols, nrow, nrhs, size), bf16),
-            dma((4,)),
+            dma((7,)),
             dma((ROUNDS - 1,)), dma((ROUNDS - 1,)), dma((ROUNDS - 1,)), dma((ROUNDS - 1,)),
             dma, dma, dma, dma, dma, dma,
         ],
         compiler_params=pltpu.CompilerParams(
-            collective_id=0, has_side_effects=True, vmem_limit_bytes=VMEM_MIB * 2**20
+            collective_id=0, has_side_effects=True, vmem_limit_bytes=int(VMEM_MIB * 2**20)
         ),
         cost_estimate=pl.CostEstimate(
             flops=2 * ROUNDS * blocks * size * size * nrhs,

time: 127 us -> 125 us (0.984)
    pallas_call x1, Pallas kernels: 124 us -> 123 us  [shards(): pl.pallas_call(functools.partial(kernel, (rows, cols, nrow, nslot, ncol))...]
where the time goes in v4:
time: 125 us
  Pallas kernels  123 us (98%)
  local copies, waits for them, and re-layouts  1.94 us (2%)
    pallas_call x1, Pallas kernels, shards(): pl.pallas_call(functools.partial(kernel, (rows, cols, nrow, nslot, ncol))...  123 us

profile of v4, /device:TPU:1, one launch (start us, length us, event | category | flops | bytes accessed | tf_op | source)
XLA Modules:
  0.0 125.4 jit_solution(17800410066863918078)
XLA Ops:
  0.6 0.0 copy-start
  0.6 0.0 copy-start.1
  0.7 0.0 copy-start.2
  0.7 0.0 copy-start.3
  0.7 0.6 copy-done
  1.3 0.0 copy-done.1
  1.3 0.0 copy-done.2
  1.3 0.0 copy-done.3
  1.3 122.7 %shard_map.86 = (f32[16,8,128]{2,1,0:T(8,128)S(1)}, f32[16,8,128]{2,1,0:T(8,128)S(1)}) custom-call(s32[256]{0:T(256)S(1)} %copy-done.2, s32[64]{0:T(128)S(1)} %copy-done.3, s32[4,8]{1,0:T(4,128)S(1)} %bitcast.4, bf16[32,128,128]{2,1,0:T(8,128)(2,1)} %bitcast.5, f32[512,128]{1,0:T(8,128)} %bitcast.6, f32[512,128]{1,0:T(8,128)} %bitcast.7, f32[8,128]{1,0:T(8,128)S(1)} %copy-done), custom_call_target="tpu_custom_call" | custom-call | flops 184549376 | bytes 2097152 | tf_op jit(solution)/shard_map/pallas_call | solution.py:316
  124.1 0.6 copy.11
  124.7 0.6 copy.12
Async XLA Ops:
  0.6 0.7 copy-start
  0.6 0.7 copy-start.1
  0.7 0.7 copy-start.2
  0.7 0.7 copy-start.3

commit v5 on v4

--- a/solution.py
+++ b/solution.py
@@ -13,7 +13,7 @@
 ROUNDS = 2 * LEVELS - 1
 SIDE, CORES = 4, 2
 FAR = 4096
-VMEM_MIB = 53.75
+VMEM_BYTES = 32 * 2**20
 
 
 def ring(d, n):
@@ -48,6 +48,21 @@
     xc = [[lax.rem(x + d, SIDE) * CORES + lax.rem(core + e, CORES) for e in range(CORES)] for d in range(SIDE)]
     zs = sorted(range(1, cols), key=lambda d: -ring(d, cols))
 
+    barrier = pltpu.get_barrier_semaphore()
+
+    def greet(to):
+        pl.semaphore_signal(barrier, inc=1, device_id=to, device_id_type=MESH)
+
+    for d in zs:
+        greet((base + col, lax.rem(col + d, cols)))
+    for _, dx, dc in LINE[:-1]:
+        greet((base + xc[dx][dc], lane))
+
+    @pl.when(off_diag)
+    def _():
+        greet((base + lane, lane))
+        greet((base + col, col))
+
     copies = [
         pltpu.make_async_copy(src, dst, sem_in.at[k])
         for k, (src, dst) in enumerate([(f_hbm, f_ref), (low_hbm, low), (up_hbm, up), (piv_hbm, piv),
@@ -55,21 +70,6 @@
     ]
     for copy in copies:
         copy.start()
-
-    barrier = pltpu.get_barrier_semaphore()
-
-    def greet(to):
-        pl.semaphore_signal(barrier, inc=1, device_id=to, device_id_type=MESH)
-
-    for d in zs:
-        greet((base + col, lax.rem(col + d, cols)))
-    for _, dx, dc in LINE[:-1]:
-        greet((base + xc[dx][dc], lane))
-
-    @pl.when(off_diag)
-    def _():
-        greet((base + lane, lane))
-        greet((base + col, col))
 
     for dy, dx, dc in PLANE[:-1]:
         greet((ys[dy] + xc[dx][dc], col))
@@ -344,17 +344,17 @@
             dma, dma, dma, dma, dma, dma,
         ],
         compiler_params=pltpu.CompilerParams(
-            collective_id=0, has_side_effects=True, vmem_limit_bytes=int(VMEM_MIB * 2**20)
+            collective_id=0, has_side_effects=True, vmem_limit_bytes=VMEM_BYTES
         ),
         cost_estimate=pl.CostEstimate(
             flops=2 * ROUNDS * blocks * size * size * nrhs,
             bytes_accessed=4 * blocks * size * size, transcendentals=0,
         ),
-    )(
+    )(*[pltpu.with_memory_space_constraint(a, pltpu.HBM) for a in (
         snode_of_block, level_of_snode, slot_columns.T,
         factor.reshape(blocks, size, size), lower_rhs.reshape(nrhs * ncol, size),
         upper_rhs.reshape(nrhs * ncol, size), inverse_pivot,
-    )
+    )])
 
 
 def solution(mesh):

time: 125 us -> 125 us (level)
  no operation moved by 1% of the time
where the time goes in v5:
time: 125 us
  Pallas kernels  123 us (98%)
  local copies, waits for them, and re-layouts  1.26 us (1%)
    pallas_call x1, Pallas kernels, shards(): pl.pallas_call(functools.partial(kernel, (rows, cols, nrow, nslot, ncol))...  123 us

profile of v5, /device:TPU:1, one launch (start us, length us, event | category | flops | bytes accessed | tf_op | source)
XLA Modules:
  0.0 124.7 jit_solution(17448733567479148730)
XLA Ops:
  0.6 122.8 %shard_map.86 = (f32[16,8,128]{2,1,0:T(8,128)S(1)}, f32[16,8,128]{2,1,0:T(8,128)S(1)}) custom-call(s32[256]{0:T(256)} %snode_hbm.1, s32[64]{0:T(128)} %level_hbm.1, s32[4,8]{1,0:T(4,128)} %bitcast.7, bf16[32,128,128]{2,1,0:T(8,128)(2,1)} %bitcast.4, f32[512,128]{1,0:T(8,128)} %bitcast.5, f32[512,128]{1,0:T(8,128)} %bitcast.6, f32[8,128]{1,0:T(8,128)} %piv_hbm.1), custom_call_target="tpu_custom_call" | custom-call | flops 184549376 | bytes 2097152 | tf_op jit(solution)/shard_map/pallas_call | solution.py:316
  123.5 0.6 copy.11
  124.1 0.6 copy.12

commit v6 on v5

--- a/solution.py
+++ b/solution.py
@@ -28,7 +28,7 @@
 
 
 def kernel(
-    dims, snode_hbm, level_hbm, slots_hbm, f_hbm, low_hbm, up_hbm, piv_hbm, low_ref, up_ref,
+    dims, snode_hbm, level_hbm, slots_hbm, f_hbm, low_hbm, up_hbm, piv_hbm, out_ref,
     snode, level, slots, tbl, rlev, f_ref, low, up, piv, f2, piv8, own_piv, held, land, psend, precv, xs, xrecv, last, zrecv,
     sem_in, send1, recv1, send2, recv2, send3, recv3, send4, recv4, send5, recv5,
 ):
@@ -254,15 +254,16 @@
         xs[0] += one(own_level == t) * sol
         xs[1] += one(own_level == TOP - t) * sol
 
-        @pl.when(t == TOP - 1)
-        def _():
-            give()
-
         spread_wait(n)
         parts(n + 1, None, lambda: None)
         w = gathered(n + 1)
         rhs = one(own_level == t + 1) * low[mine_rows, :] + one(own_level == TOP - 1 - t) * up[mine_rows, :]
         spread(n + 1, rhs - w)
+
+        @pl.when(t == TOP - 1)
+        def _():
+            give()
+
         spread_wait(n + 1)
 
     level_step(0, True)
@@ -299,8 +300,8 @@
     for i in range(nrow):
         sol = jnp.sum(zrecv[:, i].astype(jnp.float32), axis=0)
         lev = rlev[i]
-        low_ref[:, i, :] = xrecv[i, 0] + one(lev == TOP) * sol
-        up_ref[:, i, :] = xrecv[i, 1] + one(lev == 0) * sol
+        out_ref[0, :, i, :] = xrecv[i, 0] + one(lev == TOP) * sol
+        out_ref[1, :, i, :] = xrecv[i, 1] + one(lev == 0) * sol
     pltpu.make_async_copy(some, some, send4).wait()
 
 
@@ -313,11 +314,11 @@
     vmem = pl.BlockSpec(memory_space=pltpu.VMEM)
     hbm = pl.BlockSpec(memory_space=pltpu.HBM)
     dma = pltpu.SemaphoreType.DMA
-    return pl.pallas_call(
+    out = pl.pallas_call(
         functools.partial(kernel, (rows, cols, nrow, nslot, ncol)),
-        out_shape=[jax.ShapeDtypeStruct((nrhs, nrow, size), f32)] * 2,
+        out_shape=jax.ShapeDtypeStruct((2, nrhs, nrow, size), f32),
         in_specs=[hbm] * 7,
-        out_specs=[vmem, vmem],
+        out_specs=vmem,
         scratch_shapes=[
             pltpu.SMEM(snode_of_block.shape, jnp.int32),
             pltpu.SMEM(level_of_snode.shape, jnp.int32),
@@ -355,6 +356,7 @@
         factor.reshape(blocks, size, size), lower_rhs.reshape(nrhs * ncol, size),
         upper_rhs.reshape(nrhs * ncol, size), inverse_pivot,
     )])
+    return out[0], out[1]
 
 
 def solution(mesh):

time: 125 us -> 124 us (level)
    unnamed x2 -> x0, local copies, waits for them, and re-layouts: 1.26 us -> none
where the time goes in v6:
time: 124 us
  Pallas kernels  122 us (98%)
    pallas_call x1, Pallas kernels, shards(): pl.pallas_call(functools.partial(kernel, (rows, cols, nrow, nslot, ncol))...  122 us

profile of v6, /device:TPU:1, one launch (start us, length us, event | category | flops | bytes accessed | tf_op | source)
XLA Modules:
  0.0 123.7 jit_solution(17997725786522231989)
XLA Ops:
  0.6 122.4 %shard_map.86 = f32[2,16,8,128]{3,2,1,0:T(8,128)S(1)} custom-call(s32[256]{0:T(256)} %snode_hbm.1, s32[64]{0:T(128)} %level_hbm.1, s32[4,8]{1,0:T(4,128)} %bitcast.11, bf16[32,128,128]{2,1,0:T(8,128)(2,1)} %bitcast.8, f32[512,128]{1,0:T(8,128)} %bitcast.9, f32[512,128]{1,0:T(8,128)} %bitcast.10, f32[8,128]{1,0:T(8,128)} %piv_hbm.1), custom_call_target="tpu_custom_call" | custom-call | flops 184549376 | bytes 2097152 | tf_op jit(solution)/shard_map/pallas_call | solution.py:317
  123.1 0.7 slice_bitcast_fusion

commit v7 on v6

--- a/solution.py
+++ b/solution.py
@@ -166,7 +166,7 @@
 
         @pl.when(on_diag)
         def _():
-            precv[n, col] = psend[n, col]
+            pltpu.make_async_copy(psend.at[n, col], precv.at[n, col], recv1.at[n]).start()
 
     def wait_bytes(ref, count, sem):
         @pl.when(on_diag)
@@ -180,7 +180,7 @@
             pltpu.make_async_copy(part, part, sem).wait()
 
     def gathered(n):
-        wait_bytes(precv.at[n], cols, recv1.at[n])
+        pltpu.make_async_copy(precv.at[n], precv.at[n], recv1.at[n]).wait()
         return jnp.sum(precv[n].astype(jnp.float32), axis=0)
 
     def spread(n, value):

time: 124 us -> 124 us (level)
  no operation moved by 1% of the time
where the time goes in v7:
time: 124 us
  Pallas kernels  122 us (98%)
    pallas_call x1, Pallas kernels, shards(): pl.pallas_call(functools.partial(kernel, (rows, cols, nrow, nslot, ncol))...  122 us

profile of v7, /device:TPU:1, one launch (start us, length us, event | category | flops | bytes accessed | tf_op | source)
XLA Modules:
  0.0 123.6 jit_solution(11791564313316940555)
XLA Ops:
  0.6 122.3 %shard_map.86 = f32[2,16,8,128]{3,2,1,0:T(8,128)S(1)} custom-call(s32[256]{0:T(256)} %snode_hbm.1, s32[64]{0:T(128)} %level_hbm.1, s32[4,8]{1,0:T(4,128)} %bitcast.11, bf16[32,128,128]{2,1,0:T(8,128)(2,1)} %bitcast.8, f32[512,128]{1,0:T(8,128)} %bitcast.9, f32[512,128]{1,0:T(8,128)} %bitcast.10, f32[8,128]{1,0:T(8,128)} %piv_hbm.1), custom_call_target="tpu_custom_call" | custom-call | flops 184549376 | bytes 2097152 | tf_op jit(solution)/shard_map/pallas_call | solution.py:317
  122.9 0.7 slice_bitcast_fusion
